TPU v7x, 32 devices: a whole 2x2x4 slice. The times are simulated.
32 devices in a mesh: ctx: 16 (over z, y, x), mix: 2 (over core).
Axes of the slice: x: 2, y: 2, z: 4, core: 2. Of those that a mesh axis runs over, the one named last changes fastest.
Arguments:
- sources: float32 [8, 131072], P('mix', 'ctx'), may hold values from -6 to 6
- source_ids: int32 [4, 3], replicated, may hold values from 0 to 7
- mix_weights: float32 [4, 3], replicated, may hold values from 0.1 to 0.8, as said below
- source_lengths: int32 [4, 3], replicated, may hold values from 512 to 4096, as said below
- w_embed: bfloat16 [512, 32], replicated, may hold values from -1 to 1
- w_qkv: bfloat16 [512, 1536], replicated, may hold values from -0.25 to 0.25
- w_out: bfloat16 [512, 512], replicated, may hold values from -0.25 to 0.25
- forget: float32 [4, 4, 4096], P('mix', None, 'ctx'), may hold values from 0.5 to 1, as said below
- cotangent: bfloat16 [4, 4096, 512], P('mix', 'ctx'), may hold values from -0.125 to 0.125
Outputs:
- output: bfloat16 [4, 4096, 512], P('mix', 'ctx')
- grad_qkv: float32 [512, 1536], P('ctx')
- grad_out: float32 [512, 512], P('ctx')
- grad_embed: float32 [512, 32], P('ctx')
Inputs may be any that keep to these rules, and one draw needn't show every extreme that they name: `mix_weights`: each row sums to one. `source_lengths`: in every row one entry equals 4096. `forget`: below one.
All inputs are finite; a program needn't handle non-finite values.
Results may differ from a plain program's by a relative error of at most 0.015.
Values sent between devices are 32-bit elements; how exact they have to be, the bound alone decides.
No kernel may reach another device: no remote copies, remote signals or barrier semaphores. Data moves between devices by JAX's collectives and lax.ppermute only.
A program may use at most 128 MiB of HBM per device.

v0:
```python
import functools

import jax
import jax.numpy as jnp
from jax import lax
from jax.experimental import pallas as pl
from jax.experimental.pallas import tpu as pltpu
from jax.sharding import PartitionSpec as P

EPS = 1e-06
F32 = jnp.float32
BF16 = jnp.bfloat16
LEVEL_ORDERS = ((1, 2, 3), (1, 2, 3))
HEAD_ORDER = (1, 2, 3)
GROUP_ORDER = (1, 2, 3)
VMEM_LIMIT = 24 * 2**20


def quick(left, right, dims=((1,), (0,))):
    return lax.dot_general(
        left.astype(BF16), right.astype(BF16), (dims, ((), ())), preferred_element_type=F32
    )


def halves(array):
    high = array.astype(BF16)
    return high, (array - high.astype(F32)).astype(BF16)


def rows_cols(shape):
    return lax.broadcasted_iota(jnp.int32, shape, 0), lax.broadcasted_iota(jnp.int32, shape, 1)


def block_mask(heads, high, wide):
    row, col = rows_cols((heads * high, heads * wide))
    return (row // high) == (col // wide)


def stacked(array, heads):
    return jnp.concatenate([array] * heads, axis=0)


def radices(count):
    found = []
    while count > 1:
        radix = 4 if count % 4 == 0 else 2 if count % 2 == 0 else count
        found.append(radix)
        count //= radix
    return found


def other(place, radix, slot):
    if radix & (radix - 1) == 0:
        return place ^ slot
    return (place + slot) % radix


def swap(array, axis, stride, radix, slot):
    pairs = []
    for source in range(lax.axis_size(axis)):
        place = (source // stride) % radix
        for target in range(radix):
            if other(target, radix, slot) == place:
                pairs.append((source, source + (target - place) * stride))
    return lax.ppermute(array, axis, pairs)


def call(kernel, outs, ins, hbm=(), out_hbm=(), flops=0, scratch=()):
    specs = [
        pl.BlockSpec(memory_space=pltpu.HBM if i in hbm else pltpu.VMEM) for i in range(len(ins))
    ]
    ins = [
        pltpu.with_memory_space_constraint(x, pltpu.HBM) if i in hbm else x
        for i, x in enumerate(ins)
    ]
    return pl.pallas_call(
        kernel,
        out_shape=[jax.ShapeDtypeStruct(s, d) for s, d in outs],
        in_specs=specs,
        out_specs=[
            pl.BlockSpec(memory_space=pl.ANY if i in out_hbm else pltpu.VMEM)
            for i in range(len(outs))
        ],
        scratch_shapes=list(scratch),
        compiler_params=pltpu.CompilerParams(vmem_limit_bytes=VMEM_LIMIT),
        cost_estimate=pl.CostEstimate(flops=flops, bytes_accessed=1 << 20, transcendentals=0),
    )(*ins)


def rebuilt(high, low):
    top = jnp.concatenate([high, low], axis=1)
    bottom = jnp.concatenate([high, jnp.zeros_like(low)], axis=1)
    return jnp.concatenate([top, bottom], axis=0)


def pair(array):
    return jnp.concatenate(halves(array), axis=1)


def fine(left, right):
    both = quick(left, right)
    half = both.shape[1] // 2
    return both[:, :half] + both[:, half:]


def summed(array, ones):
    return quick(pair(array), ones)


def fetch(sources, targets, sems):
    copies = [
        pltpu.make_async_copy(source, target, sems.at[i])
        for i, (source, target) in enumerate(zip(sources, targets))
    ]
    for copy in copies:
        copy.start()
    return copies


def mix_kernel(held, local, patch, mixes, ids_hbm, weights_hbm, lengths_hbm, src_hbm, *rest):
    outs, (ids, weights, lengths, src, sems) = rest[:mixes], rest[mixes:]
    copies = fetch((src_hbm, ids_hbm, weights_hbm, lengths_hbm), (src, ids, weights, lengths), sems)
    me = lax.axis_index("mix")
    _, high, lanes = outs[0].shape
    first = lax.axis_index("ctx") * (high * lanes // patch)
    row, col = rows_cols((high, lanes))
    position = first + row * (lanes // patch) + col // patch
    for copy in copies:
        copy.wait()
    for slot in range(mixes):
        target = other(me, mixes, slot)
        for b in range(local):
            total = jnp.zeros((high, lanes), F32)
            for term in range(ids.shape[1]):
                mixture = target * local + b
                at = ids[mixture, term] - me * held
                here = jnp.logical_and(at >= 0, at < held)
                factor = jnp.where(here, weights[mixture, term], 0.0)
                rows = src[pl.ds(jnp.where(here, at, 0), high, held), :]
                total += jnp.where(position < lengths[mixture, term], factor, 0.0) * rows
            outs[slot][b] = total


def gate_kernel(patch, forget_hbm, gx_ref, fade_ref, row_ref, forget, sems):
    copies = fetch((forget_hbm,), (forget,), sems)
    local, heads, steps = forget.shape
    lanes = heads * patch
    s, t = rows_cols((steps, steps))
    upto = (s <= t).astype(BF16)
    for copy in copies:
        copy.wait()
    for b in range(local):
        log_gate = jnp.log1p(forget[b] - 1.0)
        high, low = halves(log_gate)
        lowest = (log_gate - high.astype(F32) - low.astype(F32)).astype(BF16)
        sums = quick(jnp.concatenate([high, low, lowest, jnp.zeros_like(low)], axis=0), upto)
        sums = sums[:heads] + sums[heads : 2 * heads] + sums[2 * heads : 3 * heads]
        row_ref[b * heads : (b + 1) * heads] = sums
        wide = jnp.broadcast_to(sums[:, None, :], (heads, patch, steps)).reshape(lanes, steps)
        gx = wide.T
        gx_ref[b] = gx
        fade_ref[b] = jnp.exp(gx[steps - 1 : steps] - gx)


def gram_kernel(heads, patch, count, *refs):
    parts, (gx, fade) = refs[:count], refs[count : count + 2]
    mt_ref, pack_ref = refs[count + 2 :]
    local, steps, lanes = gx.shape
    per = lanes // patch
    t, r = rows_cols((local * steps, local * steps // per))
    spread = (t // per == r).astype(BF16)
    t, lane = rows_cols((local * steps, lanes))
    chosen = t % per == lane // patch
    a, b_ = rows_cols((lanes, lanes))
    fold = (a % patch == b_ % patch).astype(BF16)
    total = parts[0][...]
    for part in parts[1:]:
        total = total + part[...]
    wide = quick(spread, total.reshape(local * steps // per, lanes))
    mt = quick(jnp.where(chosen, wide, 0.0), fold)
    mt_ref[...] = mt.astype(BF16).reshape(mt_ref.shape)
    pack_ref[local * patch :] = jnp.zeros((pack_ref.shape[0] - local * patch, lanes), F32)
    for b in range(local):
        own = mt[b * steps : (b + 1) * steps]
        pack_ref[b * patch : (b + 1) * patch] = quick(own[:, :patch], own * fade[b], ((0,), (0,)))
        pack_ref[local * patch + b : local * patch + b + 1] = gx[b, steps - 1 : steps]


def weight_kernel(heads, *refs):
    embed_hbm, qkv_hbm, _ = refs[:3]
    a_ref, m_ref, c_ref, k_ref, v_ref, vb_ref, own_ref, qkv_ref = refs[3:11]
    embed, qkv, tall, sems = refs[11:]
    copies = fetch((embed_hbm, qkv_hbm), (embed, qkv), sems)
    patch, width = embed.shape
    rows_out = qkv_ref.shape[0]
    ctx = lax.axis_index("ctx")
    mine = pl.ds(pl.multiple_of(ctx * rows_out, rows_out), rows_out)
    copies[0].wait()
    tall[:, :patch] = embed[...].astype(F32).T
    copies[1].wait()
    a = quick(embed[...], qkv[...])
    a_ref[...] = a
    qkv_ref[...] = qkv[mine, :]
    mask = block_mask(heads, patch, width // heads)
    query, key, value = [
        jnp.where(mask, stacked(a[:, j * width : (j + 1) * width], heads), 0.0) for j in range(3)
    ]
    across = ((1,), (1,))
    key_high, key_low = halves(key)
    value_high, value_low = halves(value)
    query_high, query_low = halves(query)
    k_ref[...] = jnp.concatenate([key_high, key_high, key_low], axis=0)
    m = quick(query_high, key_high, across) + quick(query_high, key_low, across)
    m = m + quick(query_low, key_high, across)
    m_ref[...] = rebuilt(*halves(m))
    mixed = quick(value_high, value_low, across)
    c = quick(value_high, value_high, across) + mixed + mixed.T
    c_ref[...] = rebuilt(*halves(c))
    v_ref[...] = rebuilt(*halves(stacked_heads(a[:, 2 * width :], heads)))
    vb_ref[...] = jnp.concatenate([value_high, value_low], axis=1)
    tall[:, patch : 2 * patch] = a[:, 2 * width :].T
    own_ref[...] = tall[mine, :]


def out_kernel(out_hbm, cot_hbm, vb, _, b_ref, bb_ref, out_ref, cot_ref, sems):
    copies = fetch((out_hbm, cot_hbm), (out_ref, cot_ref), sems)
    copies[0].wait()
    product = quick(vb[...], jnp.concatenate([out_ref[...], out_ref[...]], axis=0)).astype(BF16)
    b_ref[...] = product
    copies[1].wait()
    given = cot_ref[...].reshape(bb_ref.shape[0] * bb_ref.shape[1], -1)
    bb_ref[...] = quick(given, product, ((1,), (1,))).reshape(bb_ref.shape)


def spread_heads(gram, square, heads):
    return jnp.where(square, stacked(gram, heads), 0.0).astype(BF16)


def intra_kernel(heads, mt, gx, sums, m, _, z_ref, qe_ref, lead_ref, bd_ref, decay_ref, gl_ref, er_ref):
    local, steps, lanes = mt.shape
    patch = lanes // heads
    subs = bd_ref.shape[1]
    sub = steps // subs
    t, s = rows_cols((sub, heads * sub))
    causal = t >= s % sub
    row, col = rows_cols((heads * sub, lanes))
    diagonal = (row // sub == col // patch).astype(BF16)
    for b in range(local):
        query = fine(jnp.concatenate([mt[b], jnp.zeros_like(mt[b])], axis=1), m[...])
        gates = sums[b * heads : (b + 1) * heads]
        wide = jnp.broadcast_to(gates[:, None, :], (heads, sub, steps))
        wide = wide.reshape(heads * sub, steps).T
        for c in range(subs):
            rows = slice(c * sub, (c + 1) * sub)
            g = gx[b, rows]
            if c == 0:
                start = jnp.zeros((1, lanes), F32)
                gl_ref[b, c] = jnp.zeros((patch, lanes), F32)
            else:
                start = gx[b, c * sub - 1 : c * sub]
                past = mt[b, : c * sub]
                fading = past.astype(F32) * jnp.exp(start - gx[b, : c * sub])
                gl_ref[b, c] = quick(past[:, :patch], fading, ((0,), (0,)))
            er_ref[b, c] = jnp.broadcast_to(jnp.exp(start), (8, lanes))
            lead = jnp.exp(g - start)
            lead_ref[b, rows] = lead
            qe_ref[b, rows] = (query[rows] * lead).astype(BF16)
            bd = stacked(mt[b, rows], heads) * diagonal
            bd_ref[b, c] = bd
            across = jnp.concatenate([gates[h : h + 1, rows] for h in range(heads)], axis=1)
            decay = jnp.where(causal, jnp.exp(wide[rows] - across), 0.0)
            decay_ref[b, c] = decay
            scores = quick(query[rows], bd, ((1,), (1,))) * decay
            z_ref[b, rows] = quick(scores, bd)


def level(packs, place, local, patch, wanted):
    radix = len(packs)
    at = [other(place, radix, slot) for slot in range(radix)]
    totals = [pack[local * patch :] for pack in packs]
    zero = jnp.zeros_like(totals[0])
    grams = None
    total = zero
    for m in range(radix):
        if wanted == "before" and m == 0:
            continue
        power = zero
        for k in range(radix):
            if k == m or (wanted == "before" and k == 0):
                continue
            after = at[k] > at[m]
            if wanted == "before":
                after = jnp.logical_and(after, at[k] < place)
            power = power + jnp.where(after, totals[k], 0.0)
        factor = jnp.exp(power)
        if wanted == "before":
            factor = jnp.where(at[m] < place, factor, 0.0)
            total = total + jnp.where(at[m] < place, totals[m], 0.0)
        else:
            total = total + totals[m]
        terms = [factor[b : b + 1] * packs[m][b * patch : (b + 1) * patch] for b in range(local)]
        grams = terms if grams is None else [g + x for g, x in zip(grams, terms)]
    return jnp.concatenate(grams + [total], axis=0)


def joined(near, far, local, patch):
    totals = near[local * patch :]
    factor = jnp.exp(totals)
    grams = [
        near[b * patch : (b + 1) * patch] + factor[b : b + 1] * far[b * patch : (b + 1) * patch]
        for b in range(local)
    ]
    return jnp.concatenate(grams + [totals + far[local * patch :]], axis=0)


def ordered(radix, order):
    return order if radix == 4 else tuple(range(1, radix))


def level_order(number, radix):
    return ordered(radix, LEVEL_ORDERS[min(number, len(LEVEL_ORDERS) - 1)])


def in_slots(packs, number):
    order = (0,) + level_order(number, len(packs))
    return [packs[order.index(slot)] for slot in range(len(packs))]


def level_kernel(local, patch, stride, radix, number, *refs):
    place = (lax.axis_index("ctx") // stride) % radix
    packs = in_slots([ref[...] for ref in refs[:radix]], number)
    before = level(packs, place, local, patch, "before")
    if number > 0:
        before = joined(refs[radix][...], before, local, patch)
    refs[-2][...] = level(packs, place, local, patch, "whole")
    refs[-1][...] = before


def main_kernel(heads, stride, radix, number, mixes, *refs):
    count = radix + int(number > 0)
    packs = in_slots([ref[...] for ref in refs[:radix]], number)
    mt, lead, bd, decay, intra, qe, gl, er, bb, c, big_b, v, w_out, cot = refs[count : count + 14]
    out_hbm, *part_refs = refs[count + 14 : -3]
    z_scr, out_scr, sems = refs[-3:]
    local, steps, lanes = mt.shape
    patch = lanes // heads
    subs = bd.shape[1]
    sub = steps // subs
    width = w_out.shape[0]
    size = width // heads
    place = (lax.axis_index("ctx") // stride) % radix
    state = level(packs, place, local, patch, "before")
    if number > 0:
        state = joined(refs[radix][...], state, local, patch)
    square = block_mask(heads, patch, patch)
    ones = jnp.concatenate([square.astype(BF16)] * 2, axis=0)
    places = [(b, i) for b in range(local) for i in range(subs)]
    grams = []
    z = []
    for b, i in places:
        gram = gl[b, i] + er[b, i, :1] * state[b * patch : (b + 1) * patch]
        grams.append(spread_heads(gram, square, heads))
        rows = slice(i * sub, (i + 1) * sub)
        z.append(intra[b, rows] + quick(qe[b, rows], grams[-1]))
    z = jnp.concatenate(z, axis=0)
    every = (local * steps, lanes)
    around = bb[...].reshape(every)
    met = summed(z * around, ones)
    zc = fine(pair(z), c[...])
    irms = lax.rsqrt(summed(z * zc, ones) * (1.0 / size) + EPS)
    zn = z * irms
    znb = zn.astype(BF16)
    out_scr[...] = quick(znb, big_b[...]).astype(BF16).reshape(out_scr.shape)
    leaving = fetch((out_scr,), (out_hbm,), sems)
    aligned = met * (irms * (1.0 / size))
    u = irms * (around - aligned * (irms * zc))
    ub = u.astype(BF16)
    ue = (u * lead[...].reshape(every)).astype(BF16)
    y = []
    for (b, i), gram in zip(places, grams):
        rows = slice(b * steps + i * sub, b * steps + (i + 1) * sub)
        scores = (quick(ub[rows], bd[b, i], ((1,), (1,))) * decay[b, i]).astype(BF16)
        left = jnp.concatenate([scores, ue[rows]], axis=1)
        y.append(quick(left, jnp.concatenate([bd[b, i], gram], axis=0)))
    y = jnp.concatenate(y, axis=0)
    given = cot[...].reshape(local * steps, width)
    x_total = quick(mt[...].reshape(every)[:, :patch], y, ((0,), (0,)))
    right = jnp.concatenate([given, (aligned * zn).astype(BF16)], axis=1)
    zw_total = quick(znb, right, ((0,), (0,)))
    big_z = zw_total[:, :width]
    w_total = jnp.where(square, zw_total[:, width:], 0.0)
    y_total = -fine(pair(w_total), v[...])
    y_rows = []
    for h in range(heads):
        rows = slice(h * patch, (h + 1) * patch)
        both = jnp.concatenate(halves(big_z[rows]), axis=0)
        found = quick(both, w_out[h * size : (h + 1) * size], ((1,), (1,)))
        y_rows.append(y_total[rows] + found[:patch] + found[patch:])
    y_total = jnp.concatenate(y_rows, axis=0)
    per = lax.axis_size("ctx") // heads
    head = lax.axis_index("ctx") // per
    me = lax.axis_index("mix")
    panels = width // 128
    share = panels // mixes
    for k in range(panels):
        z_scr[k] = big_z[:, k * 128 : (k + 1) * 128]
    y_high = lanes // mixes
    x_high = patch // mixes
    z_scr[panels] = y_total
    z_scr[panels + 1, :patch] = x_total
    for slot in range(mixes):
        part = other(me, mixes, slot)
        out = part_refs[slot]
        at = 0
        for q in range(heads):
            for k in range(share):
                rows = pl.ds(other(head, heads, q) * patch, patch)
                out[at : at + patch] = z_scr[part * share + k, rows, :]
                at += patch
        out[at : at + y_high] = z_scr[panels, pl.ds(part * y_high, y_high), :]
        at += y_high
        out[at : at + x_high] = z_scr[panels + 1, pl.ds(part * x_high, x_high), :]
    for copy in leaving:
        copy.wait()


def stacked_heads(array, heads):
    size = array.shape[1] // heads
    return jnp.concatenate([array[:, h * size : (h + 1) * size] for h in range(heads)], axis=0)


def final_kernel(heads, mixes, *refs):
    parts = refs[:mixes]
    a, keys, own, qkv_rows = refs[mixes : mixes + 4]
    gq_ref, go_ref, ge_ref, scr = refs[mixes + 4 :]
    patch = ge_ref.shape[1]
    width = go_ref.shape[1]
    size = width // heads
    lanes = heads * patch
    panels = width // 128
    share = panels // mixes
    y_high = lanes // mixes
    x_high = patch // mixes
    me = lax.axis_index("mix")
    for slot in range(mixes):
        part = other(me, mixes, slot)
        at = 0
        for k in range(share):
            scr[part * share + k, :patch] = parts[slot][at : at + patch]
            at += patch
        scr[panels, pl.ds(part * y_high, y_high), :] = parts[slot][at : at + y_high]
        at += y_high
        scr[panels + 1, pl.ds(part * x_high, x_high), :] = parts[slot][at : at + x_high]
    y = scr[panels]
    x_high, x_low = halves(scr[panels + 1, :patch])
    t_query = quick(jnp.concatenate([x_high, x_low, x_high], axis=1), keys[...])
    query_high, query_low = halves(a[:, :width])
    crossed = quick(
        jnp.concatenate([x_high, x_low, x_high], axis=0),
        jnp.concatenate([query_high, query_high, query_low], axis=0),
        ((0,), (0,)),
    )
    t_key = [crossed[h * patch : (h + 1) * patch, h * size : (h + 1) * size] for h in range(heads)]
    t_value = [y[h * patch : (h + 1) * patch] for h in range(heads)]
    t = jnp.concatenate([t_query] + t_key + t_value, axis=1)
    high, low = halves(t)
    both = jnp.concatenate([high, low], axis=0)
    embed_rows = own[:, :patch].astype(BF16)
    gq_ref[...] = quick(jnp.concatenate([embed_rows, embed_rows], axis=1), both)
    found = quick(qkv_rows[...], both, ((1,), (1,)))
    ge_ref[...] = found[:, :patch] + found[:, patch:]
    v_high, v_low = halves(own[:, patch : 2 * patch])
    z_high, z_low = halves(jnp.concatenate([scr[k, :patch] for k in range(panels)], axis=1))
    go_ref[...] = quick(
        jnp.concatenate([v_high, v_low, v_high], axis=1),
        jnp.concatenate([z_high, z_high, z_low], axis=0),
    )


def slot_kernel(heads, z_high, *refs):
    parts, slots = refs[:-heads], refs[-heads:]
    total = parts[0][...]
    for part in parts[1:]:
        total = total + part[...]
    for q in range(heads):
        slots[q][:z_high] = total[q * z_high : (q + 1) * z_high]
        slots[q][z_high:] = total[heads * z_high :]


def add_kernel(*refs):
    total = refs[0][...]
    for ref in refs[1:-1]:
        total = total + ref[...]
    refs[-1][...] = total


def added(arrays):
    (total,) = call(add_kernel, [(arrays[0].shape, F32)], arrays)
    return total


def shards(
    sources, source_ids, mix_weights, source_lengths, w_embed, w_qkv, w_out, forget, cotangent
):
    mixes = lax.axis_size("mix")
    count = lax.axis_size("ctx")
    patch = w_embed.shape[1]
    local, heads, steps = forget.shape
    width = w_out.shape[0]
    size = width // heads
    lanes = heads * patch
    held = sources.shape[0]
    rows_out = width // count
    per = count // heads
    dma = pltpu.SemaphoreType.DMA
    partial_shape = (local, steps * patch // lanes, lanes)
    panels = sources.reshape((held,) + partial_shape[1:]).transpose(1, 0, 2).reshape(-1, lanes)
    partials = call(
        functools.partial(mix_kernel, held, local, patch, mixes),
        [(partial_shape, F32)] * mixes,
        [source_ids, mix_weights, source_lengths, panels],
        hbm=(0, 1, 2, 3),
        scratch=[
            pltpu.SMEM(source_ids.shape, jnp.int32),
            pltpu.SMEM(mix_weights.shape, F32),
            pltpu.SMEM(source_lengths.shape, jnp.int32),
            pltpu.VMEM(panels.shape, F32),
            dma((4,)),
        ],
    )
    got = [partials[0]] + [swap(partials[s], "mix", 1, mixes, s) for s in range(1, mixes)]
    subs = heads
    sub = steps // subs
    gx, fade, sums = call(
        functools.partial(gate_kernel, patch),
        [((local, steps, lanes), F32), ((local, steps, lanes), F32), ((local * heads, steps), F32)],
        [forget],
        hbm=(0,),
        flops=10**8,
        scratch=[pltpu.VMEM(forget.shape, F32), dma((1,))],
    )
    high = -(-local // 8) * 8
    pack_shape = ((local * patch + high, lanes), F32)
    mt, pack = call(
        functools.partial(gram_kernel, heads, patch, mixes),
        [((local, steps, lanes), BF16), pack_shape],
        got + [gx, fade],
    )
    a, m, c, keys, v, value_blocks, own, qkv_rows = call(
        functools.partial(weight_kernel, heads),
        [
            ((patch, 3 * width), F32),
            ((2 * lanes, 2 * lanes), BF16),
            ((2 * lanes, 2 * lanes), BF16),
            ((3 * lanes, width), BF16),
            ((2 * lanes, 2 * size), BF16),
            ((lanes, 2 * width), BF16),
            ((rows_out, 2 * patch), F32),
            ((rows_out, 3 * width), BF16),
        ],
        [w_embed.T, w_qkv, pack],
        hbm=(0, 1),
        flops=10**9,
        scratch=[
            pltpu.VMEM((patch, width), BF16),
            pltpu.VMEM(w_qkv.shape, BF16),
            pltpu.VMEM((width, 2 * patch), F32),
            dma((2,)),
        ],
    )
    steps_up = radices(count)
    stride = 1
    near = []
    for i, radix in enumerate(steps_up):
        order = level_order(i, radix)
        packs = [pack] + [swap(pack, "ctx", stride, radix, s) for s in order]
        if i == len(steps_up) - 1:
            break
        pack, before = call(
            functools.partial(level_kernel, local, patch, stride, radix, i),
            [pack_shape] * 2,
            packs + near,
        )
        near = [before]
        stride *= radix
    intra, qe, lead, bd, decay, gl, er = call(
        functools.partial(intra_kernel, heads),
        [
            ((local, steps, lanes), F32),
            ((local, steps, lanes), BF16),
            ((local, steps, lanes), F32),
            ((local, subs, heads * sub, lanes), BF16),
            ((local, subs, sub, heads * sub), F32),
            ((local, subs, patch, lanes), F32),
            ((local, subs, 8, lanes), F32),
        ],
        [mt, gx, sums, m, pack],
        flops=10**9,
    )
    big_b, bb, w_out_near, cot_near = call(
        out_kernel,
        [
            ((lanes, width), BF16),
            ((local, steps, lanes), F32),
            (w_out.shape, BF16),
            (cotangent.shape, BF16),
        ],
        [w_out, cotangent, value_blocks, pack],
        hbm=(0, 1),
        flops=10**9,
        scratch=[dma((2,))],
    )
    part_rows = heads * (width // 128 // mixes) * patch + lanes // mixes + patch // mixes
    output, *parts = call(
        functools.partial(main_kernel, heads, stride, radix, i, mixes),
        [((local, steps, width), BF16)] + [((part_rows, 128), F32)] * mixes,
        packs + near + [mt, lead, bd, decay, intra, qe, gl, er, bb, c, big_b, v, w_out_near, cot_near],
        flops=10**9,
        out_hbm=(0,),
        scratch=[
            pltpu.VMEM((width // 128 + 2, lanes, 128), F32),
            pltpu.VMEM((local, steps, width), BF16),
            dma((1,)),
        ],
    )
    z_high = (width // 128 // mixes) * patch
    y_high = part_rows - heads * z_high
    slots = call(
        functools.partial(slot_kernel, heads, z_high),
        [((z_high + y_high, 128), F32)] * heads,
        [parts[0]] + [swap(parts[s], "mix", 1, mixes, s) for s in range(1, mixes)],
    )
    order = ordered(heads, HEAD_ORDER)
    both = added([slots[0]] + [swap(slots[s], "ctx", per, heads, s) for s in order])
    stride = 1
    for radix in radices(per):
        order = ordered(radix, GROUP_ORDER)
        both = added([both] + [swap(both, "ctx", stride, radix, s) for s in order])
        stride *= radix
    pieces = [both] + [swap(both, "mix", 1, mixes, s) for s in range(1, mixes)]
    grads = call(
        functools.partial(final_kernel, heads, mixes),
        [((rows_out, 3 * width), F32), ((rows_out, width), F32), ((rows_out, patch), F32)],
        pieces + [a, keys, own, qkv_rows],
        scratch=[pltpu.VMEM((width // 128 + 2, lanes, 128), F32)],
    )
    return output, grads[0], grads[1], grads[2]


def solution(mesh):
    placed = (
        P("mix", "ctx"),
        P(),
        P(),
        P(),
        P(),
        P(),
        P(),
        P("mix", None, "ctx"),
        P("mix", "ctx", None),
    )
    return jax.shard_map(
        shards,
        mesh=mesh,
        in_specs=placed,
        out_specs=(P("mix", "ctx", None), P("ctx", None), P("ctx", None), P("ctx", None)),
        check_vma=False,
    )
```

profile of v0, /device:TPU:0, one launch (start us, length us, event | category | flops | bytes accessed | tf_op | source)
XLA Modules:
  0.0 41.8 jit_solution(8081772656483659980)
XLA Ops:
  0.6 1.0 %shard_map.120 = (f32[2,64,128]{2,1,0:T(8,128)S(1)}, f32[2,64,128]{2,1,0:T(8,128)S(1)}) custom-call(s32[4,3]{1,0:T(4,128)} %ids_hbm.1, f32[4,3]{1,0:T(4,128)} %weights_hbm.1, s32[4,3]{1,0:T(4,128)} %lengths_hbm.1, f32[256,128]{1,0:T(8,128)} %bitcast.6), custom_call_target="tpu_custom_call" | custom-call | bytes 1048576 | tf_op jit(solution)/shard_map/pallas_call | solution.py:76
  1.7 0.5 %collective-permute-start = (f32[2,64,128]{2,1,0:T(8,128)S(1)}, f32[2,64,128]{2,1,0:T(8,128)S(1)}, u32[]{:S(2)}, u32[]{:S(2)}) collective-permute-start(f32[2,64,128]{2,1,0:T(8,128)S(1)} %get-tuple-element.43), channel_id=1, source_target_pairs={{0,1},{1,0},{2,3},{3,2},{4,5},{5,4},{6,7},{7,6},{8,9},{9,8},{10,11... | collective-permute-start | bytes 196616 | tf_op jit(solution)/shard_map/ppermute | solution.py:65
  2.2 1.0 %shard_map.121 = (f32[2,256,128]{2,1,0:T(8,128)S(1)}, f32[2,256,128]{2,1,0:T(8,128)S(1)}, f32[8,256]{1,0:T(8,128)S(1)}) custom-call(f32[2,4,256]{2,1,0:T(4,128)} %forget_hbm.1), custom_call_target="tpu_custom_call" | custom-call | flops 100000000 | bytes 1048576 | tf_op jit(solution)/shard_map/pallas_call | solution.py:76
  3.7 3.7 %collective-permute-start.3 = (f32[72,128]{1,0:T(8,128)S(1)}, f32[72,128]{1,0:T(8,128)S(1)}, u32[]{:S(2)}, u32[]{:S(2)}) collective-permute-start(f32[72,128]{1,0:T(8,128)S(1)} %get-tuple-element.46.refs_0_.refs_2_), channel_id=1, source_target_pairs={{0,6},{2,4},{4,2},{6,0},{8,14},{10,12},{12,10},{14,8},{16,22},{18,... | collective-permute-start | bytes 110600 | tf_op jit(solution)/shard_map/ppermute | solution.py:65
  7.4 0.5 %collective-permute-start.2 = (f32[72,128]{1,0:T(8,128)S(1)}, f32[72,128]{1,0:T(8,128)S(1)}, u32[]{:S(2)}, u32[]{:S(2)}) collective-permute-start(f32[72,128]{1,0:T(8,128)S(1)} %get-tuple-element.46.refs_0_.refs_2_), channel_id=1, source_target_pairs={{0,4},{2,6},{4,0},{6,2},{8,12},{10,14},{12,8},{14,10},{16,20},{18,... | collective-permute-start | bytes 110600 | tf_op jit(solution)/shard_map/ppermute | solution.py:65
  8.1 2.2 %shard_map.124 = (f32[32,1536]{1,0:T(8,128)S(1)}, bf16[256,256]{1,0:T(8,128)(2,1)S(1)}, bf16[256,256]{1,0:T(8,128)(2,1)S(1)}, bf16[384,512]{1,0:T(8,128)(2,1)S(1...) custom-call(bf16[32,512]{1,0:T(8,128)(2,1)} %bitcast.7, ...), custom_call_target="tpu_custom_call" | custom-call | flops 1000000000 | bytes 1048576 | tf_op jit(solution)/shard_map/pallas_call | solution.py:76
  10.3 1.1 %collective-permute-done.2.refs_2_ = f32[72,128]{1,0:T(8,128)S(1)} collective-permute-done((f32[72,128]{1,0:T(8,128)S(1)}, f32[72,128]{1,0:T(8,128)S(1)}, u32[]{:S(2)}, u32[]{:S(2)}) %collective-permute-start.2) | collective-permute-done | bytes 36896 | tf_op jit(solution)/shard_map/ppermute | solution.py:65
  11.9 3.7 %collective-permute-start.6 = (f32[72,128]{1,0:T(8,128)S(1)}, f32[72,128]{1,0:T(8,128)S(1)}, u32[]{:S(2)}, u32[]{:S(2)}) collective-permute-start(f32[72,128]{1,0:T(8,128)S(1)} %get-tuple-element.47._.refs_0_), channel_id=1, source_target_pairs={{0,24},{2,26},{4,28},{6,30},{8,16},{10,18},{12,20},{14,22},{16,8},... | collective-permute-start | bytes 110600 | tf_op jit(solution)/shard_map/ppermute | solution.py:65
  15.6 0.8 %collective-permute-start.4 = (f32[72,128]{1,0:T(8,128)S(1)}, f32[72,128]{1,0:T(8,128)S(1)}, u32[]{:S(2)}, u32[]{:S(2)}) collective-permute-start(f32[72,128]{1,0:T(8,128)S(1)} %get-tuple-element.47._.refs_0_), channel_id=1, source_target_pairs={{0,8},{2,10},{4,12},{6,14},{8,0},{10,2},{12,4},{14,6},{16,24},{18,... | collective-permute-start | bytes 110600 | tf_op jit(solution)/shard_map/ppermute | solution.py:65
  16.4 1.7 %shard_map.126 = (bf16[128,512]{1,0:T(8,128)(2,1)S(1)}, f32[2,256,128]{2,1,0:T(8,128)S(1)}, bf16[512,512]{1,0:T(8,128)(2,1)S(1)}, bf16[2,256,512]{2,1,0:T(8,128)(2,1)S(1)}) custom-call(bf16[512,512]{1,0:T(8,128)(2,1)} %out_hbm.1, bf16[2,256,512]{2,1,0:T(8,128)(2,1)} %cot_hbm.1, bf16[128,1024]{1,0:T(8,128)(2,1)S(1)} %get-tuple-element.59.vb, ...), custom_call_target="tpu_custom_call" | custom-call | flops 1000000000 | bytes 1048576 | tf_op jit(solution)/shard_map/pallas_call | solution.py:76
  18.1 0.9 %shard_map.125 = (f32[2,256,128]{2,1,0:T(8,128)S(1)}, bf16[2,256,128]{2,1,0:T(8,128)(2,1)S(1)}, f32[2,256,128]{2,1,0:T(8,128)S(1)}, bf16[2,4,256,128]{3,2,1,0:T(...) custom-call(bf16[2,256,128]{2,1,0:T(8,128)(2,1)S(1)} %get-tuple-element., ...), custom_call_target="tpu_custom_call" | custom-call | flops 1000000000 | bytes 1048576 | tf_op jit(solution)/shard_map/pallas_call | solution.py:76
  19.0 1.5 %collective-permute-done.5.refs_2_ = f32[72,128]{1,0:T(8,128)S(1)} collective-permute-done((f32[72,128]{1,0:T(8,128)S(1)}, f32[72,128]{1,0:T(8,128)S(1)}, u32[]{:S(2)}, u32[]{:S(2)}) %collective-permute-start.5) | collective-permute-done | bytes 36896 | tf_op jit(solution)/shard_map/ppermute | solution.py:65
  20.5 1.8 %shard_map.127 = (bf16[2,256,512]{2,1,0:T(8,128)(2,1)}, f32[336,128]{1,0:T(8,128)S(1)}, f32[336,128]{1,0:T(8,128)S(1)}) custom-call(f32[72,128]{1,0:T(8,128)S(1)} %get-tuple-element.47._.refs_0_, f32[72,128]{1,0:T(8,128)S(1)} %collective-permute-done.4.refs_1_, f32[72,128]{1,0:T(8,128)S(1)} %collective-permute-done.5.refs_2_, ...), custom_call_target="tpu_custom_call" | custom-call | flops 1000000000 | bytes 1048576 | tf_op jit(solution)/shard_map/pallas_call | solution.py:76
  22.4 1.4 %collective-permute-done.7.refs_1_ = f32[336,128]{1,0:T(8,128)S(1)} collective-permute-done((f32[336,128]{1,0:T(8,128)S(1)}, f32[336,128]{1,0:T(8,128)S(1)}, u32[]{:S(2)}, u32[]{:S(2)}) %collective-permute-start.7) | collective-permute-done | bytes 172064 | tf_op jit(solution)/shard_map/ppermute | solution.py:65
  23.9 2.7 %collective-permute-start.9 = (f32[144,128]{1,0:T(8,128)S(1)}, f32[144,128]{1,0:T(8,128)S(1)}, u32[]{:S(2)}, u32[]{:S(2)}) collective-permute-start(f32[144,128]{1,0:T(8,128)S(1)} %get-tuple-element.71), channel_id=1, source_target_pairs={{0,16},{2,18},{4,20},{6,22},{8,24},{10,26},{12,28},{14,30},{16,0},... | collective-permute-start | bytes 221192 | tf_op jit(solution)/shard_map/ppermute | solution.py:65
  26.6 1.6 %collective-permute-start.10 = (f32[144,128]{1,0:T(8,128)S(1)}, f32[144,128]{1,0:T(8,128)S(1)}, u32[]{:S(2)}, u32[]{:S(2)}) collective-permute-start(f32[144,128]{1,0:T(8,128)S(1)} %get-tuple-element.72), channel_id=1, source_target_pairs={{0,24},{2,26},{4,28},{6,30},{8,16},{10,18},{12,20},{14,22},{16,8},... | collective-permute-start | bytes 221192 | tf_op jit(solution)/shard_map/ppermute | solution.py:65
  28.3 1.5 %collective-permute-done.8.refs_1_ = f32[144,128]{1,0:T(8,128)S(1)} collective-permute-done((f32[144,128]{1,0:T(8,128)S(1)}, f32[144,128]{1,0:T(8,128)S(1)}, u32[]{:S(2)}, u32[]{:S(2)}) %collective-permute-start.8) | collective-permute-done | bytes 73760 | tf_op jit(solution)/shard_map/ppermute | solution.py:65
  29.8 3.1 %collective-permute-done.10.refs_3_ = f32[144,128]{1,0:T(8,128)S(1)} collective-permute-done((f32[144,128]{1,0:T(8,128)S(1)}, f32[144,128]{1,0:T(8,128)S(1)}, u32[]{:S(2)}, u32[]{:S(2)}) %collective-permute-start.10) | collective-permute-done | bytes 73760 | tf_op jit(solution)/shard_map/ppermute | solution.py:65
  32.9 1.6 %collective-permute-start.13 = (f32[144,128]{1,0:T(8,128)S(1)}, f32[144,128]{1,0:T(8,128)S(1)}, u32[]{:S(2)}, u32[]{:S(2)}) collective-permute-start(f32[144,128]{1,0:T(8,128)S(1)} %shard_map.129.refs_0_), channel_id=1, source_target_pairs={{0,6},{2,4},{4,2},{6,0},{8,14},{10,12},{12,10},{14,8},{16,22},{18,... | collective-permute-start | bytes 221192 | tf_op jit(solution)/shard_map/ppermute | solution.py:65
  35.0 1.5 %collective-permute-start.11 = (f32[144,128]{1,0:T(8,128)S(1)}, f32[144,128]{1,0:T(8,128)S(1)}, u32[]{:S(2)}, u32[]{:S(2)}) collective-permute-start(f32[144,128]{1,0:T(8,128)S(1)} %shard_map.129.refs_0_), channel_id=1, source_target_pairs={{0,2},{2,0},{4,6},{6,4},{8,10},{10,8},{12,14},{14,12},{16,18},{18,... | collective-permute-start | bytes 221192 | tf_op jit(solution)/shard_map/ppermute | solution.py:65
  36.5 2.2 %collective-permute-done.13.refs_3_ = f32[144,128]{1,0:T(8,128)S(1)} collective-permute-done((f32[144,128]{1,0:T(8,128)S(1)}, f32[144,128]{1,0:T(8,128)S(1)}, u32[]{:S(2)}, u32[]{:S(2)}) %collective-permute-start.13) | collective-permute-done | bytes 73760 | tf_op jit(solution)/shard_map/ppermute | solution.py:65
  38.7 0.6 %collective-permute-done.12.refs_2_ = f32[144,128]{1,0:T(8,128)S(1)} collective-permute-done((f32[144,128]{1,0:T(8,128)S(1)}, f32[144,128]{1,0:T(8,128)S(1)}, u32[]{:S(2)}, u32[]{:S(2)}) %collective-permute-start.12) | collective-permute-done | bytes 73760 | tf_op jit(solution)/shard_map/ppermute | solution.py:65
  39.4 1.3 %collective-permute-done.14.refs_1_ = f32[144,128]{1,0:T(8,128)S(1)} collective-permute-done((f32[144,128]{1,0:T(8,128)S(1)}, f32[144,128]{1,0:T(8,128)S(1)}, u32[]{:S(2)}, u32[]{:S(2)}) %collective-permute-start.14) | collective-permute-done | bytes 73760 | tf_op jit(solution)/shard_map/ppermute | solution.py:65
  40.7 1.1 %shard_map.131 = (f32[32,1536]{1,0:T(8,128)}, f32[32,512]{1,0:T(8,128)}, f32[32,32]{1,0:T(8,128)}) custom-call(f32[144,128]{1,0:T(8,128)S(1)} %shard_map.130.refs_0_, f32[144,128]{1,0:T(8,128)S(1)} %collective-permute-done.14.refs_1_, f32[32,1536]{1,0:T(8,128)S(1)} %get-tuple-element.73.refs_2_, bf16[384,512]{1,0:T(8,128)(2,1)S(1)} %get-tuple-element.74.refs_3_, ...), custom_call_target="tpu_custom_call" | custom-call | bytes 1048576 | tf_op jit(solution)/shard_map/pallas_call | solution.py:76
  (18 shorter events, 2.0 us)
Async XLA Ops:
  1.7 1.5 %collective-permute-start = (f32[2,64,128]{2,1,0:T(8,128)S(1)}, f32[2,64,128]{2,1,0:T(8,128)S(1)}, u32[]{:S(2)}, u32[]{:S(2)}) collective-permute-start(f32[2,64,128]{2,1,0:T(8,128)S(1)} %get-tuple-element.43), channel_id=1, source_target_pairs={{0,1},{1,0},{2,3},{3,2},{4,5},{5,4},{6,7},{7,6},{8,9},{9,8},{10,11... | collective-permute-start | bytes 196616 | tf_op jit(solution)/shard_map/ppermute | solution.py:65
  3.7 6.6 %collective-permute-start.3 = (f32[72,128]{1,0:T(8,128)S(1)}, f32[72,128]{1,0:T(8,128)S(1)}, u32[]{:S(2)}, u32[]{:S(2)}) collective-permute-start(f32[72,128]{1,0:T(8,128)S(1)} %get-tuple-element.46.refs_0_.refs_2_), channel_id=1, source_target_pairs={{0,6},{2,4},{4,2},{6,0},{8,14},{10,12},{12,10},{14,8},{16,22},{18,... | collective-permute-start | bytes 110600 | tf_op jit(solution)/shard_map/ppermute | solution.py:65
  7.4 4.0 %collective-permute-start.2 = (f32[72,128]{1,0:T(8,128)S(1)}, f32[72,128]{1,0:T(8,128)S(1)}, u32[]{:S(2)}, u32[]{:S(2)}) collective-permute-start(f32[72,128]{1,0:T(8,128)S(1)} %get-tuple-element.46.refs_0_.refs_2_), channel_id=1, source_target_pairs={{0,4},{2,6},{4,0},{6,2},{8,12},{10,14},{12,8},{14,10},{16,20},{18,... | collective-permute-start | bytes 110600 | tf_op jit(solution)/shard_map/ppermute | solution.py:65
  7.9 4.0 %collective-permute-start.1 = (f32[72,128]{1,0:T(8,128)S(1)}, f32[72,128]{1,0:T(8,128)S(1)}, u32[]{:S(2)}, u32[]{:S(2)}) collective-permute-start(f32[72,128]{1,0:T(8,128)S(1)} %get-tuple-element.46.refs_0_.refs_2_), channel_id=1, source_target_pairs={{0,2},{2,0},{4,6},{6,4},{8,10},{10,8},{12,14},{14,12},{16,18},{18,... | collective-permute-start | bytes 110600 | tf_op jit(solution)/shard_map/ppermute | solution.py:65
  11.9 7.1 %collective-permute-start.6 = (f32[72,128]{1,0:T(8,128)S(1)}, f32[72,128]{1,0:T(8,128)S(1)}, u32[]{:S(2)}, u32[]{:S(2)}) collective-permute-start(f32[72,128]{1,0:T(8,128)S(1)} %get-tuple-element.47._.refs_0_), channel_id=1, source_target_pairs={{0,24},{2,26},{4,28},{6,30},{8,16},{10,18},{12,20},{14,22},{16,8},... | collective-permute-start | bytes 110600 | tf_op jit(solution)/shard_map/ppermute | solution.py:65
  15.6 4.9 %collective-permute-start.5 = (f32[72,128]{1,0:T(8,128)S(1)}, f32[72,128]{1,0:T(8,128)S(1)}, u32[]{:S(2)}, u32[]{:S(2)}) collective-permute-start(f32[72,128]{1,0:T(8,128)S(1)} %get-tuple-element.47._.refs_0_), channel_id=1, source_target_pairs={{0,16},{2,18},{4,20},{6,22},{8,24},{10,26},{12,28},{14,30},{16,0},... | collective-permute-start | bytes 110600 | tf_op jit(solution)/shard_map/ppermute | solution.py:65
  15.6 4.9 %collective-permute-start.4 = (f32[72,128]{1,0:T(8,128)S(1)}, f32[72,128]{1,0:T(8,128)S(1)}, u32[]{:S(2)}, u32[]{:S(2)}) collective-permute-start(f32[72,128]{1,0:T(8,128)S(1)} %get-tuple-element.47._.refs_0_), channel_id=1, source_target_pairs={{0,8},{2,10},{4,12},{6,14},{8,0},{10,2},{12,4},{14,6},{16,24},{18,... | collective-permute-start | bytes 110600 | tf_op jit(solution)/shard_map/ppermute | solution.py:65
  22.3 1.5 %collective-permute-start.7 = (f32[336,128]{1,0:T(8,128)S(1)}, f32[336,128]{1,0:T(8,128)S(1)}, u32[]{:S(2)}, u32[]{:S(2)}) collective-permute-start(f32[336,128]{1,0:T(8,128)S(1)} %get-tuple-element.68), channel_id=1, source_target_pairs={{0,1},{1,0},{2,3},{3,2},{4,5},{5,4},{6,7},{7,6},{8,9},{9,8},{10,11... | collective-permute-start | bytes 516104 | tf_op jit(solution)/shard_map/ppermute | solution.py:65
  23.8 6.0 %collective-permute-start.8 = (f32[144,128]{1,0:T(8,128)S(1)}, f32[144,128]{1,0:T(8,128)S(1)}, u32[]{:S(2)}, u32[]{:S(2)}) collective-permute-start(f32[144,128]{1,0:T(8,128)S(1)} %get-tuple-element.70), channel_id=1, source_target_pairs={{0,8},{2,10},{4,12},{6,14},{8,0},{10,2},{12,4},{14,6},{16,24},{18,... | collective-permute-start | bytes 221192 | tf_op jit(solution)/shard_map/ppermute | solution.py:65
  23.9 5.9 %collective-permute-start.9 = (f32[144,128]{1,0:T(8,128)S(1)}, f32[144,128]{1,0:T(8,128)S(1)}, u32[]{:S(2)}, u32[]{:S(2)}) collective-permute-start(f32[144,128]{1,0:T(8,128)S(1)} %get-tuple-element.71), channel_id=1, source_target_pairs={{0,16},{2,18},{4,20},{6,22},{8,24},{10,26},{12,28},{14,30},{16,0},... | collective-permute-start | bytes 221192 | tf_op jit(solution)/shard_map/ppermute | solution.py:65
  26.6 6.3 %collective-permute-start.10 = (f32[144,128]{1,0:T(8,128)S(1)}, f32[144,128]{1,0:T(8,128)S(1)}, u32[]{:S(2)}, u32[]{:S(2)}) collective-permute-start(f32[144,128]{1,0:T(8,128)S(1)} %get-tuple-element.72), channel_id=1, source_target_pairs={{0,24},{2,26},{4,28},{6,30},{8,16},{10,18},{12,20},{14,22},{16,8},... | collective-permute-start | bytes 221192 | tf_op jit(solution)/shard_map/ppermute | solution.py:65
  32.9 5.8 %collective-permute-start.13 = (f32[144,128]{1,0:T(8,128)S(1)}, f32[144,128]{1,0:T(8,128)S(1)}, u32[]{:S(2)}, u32[]{:S(2)}) collective-permute-start(f32[144,128]{1,0:T(8,128)S(1)} %shard_map.129.refs_0_), channel_id=1, source_target_pairs={{0,6},{2,4},{4,2},{6,0},{8,14},{10,12},{12,10},{14,8},{16,22},{18,... | collective-permute-start | bytes 221192 | tf_op jit(solution)/shard_map/ppermute | solution.py:65
  34.5 4.8 %collective-permute-start.12 = (f32[144,128]{1,0:T(8,128)S(1)}, f32[144,128]{1,0:T(8,128)S(1)}, u32[]{:S(2)}, u32[]{:S(2)}) collective-permute-start(f32[144,128]{1,0:T(8,128)S(1)} %shard_map.129.refs_0_), channel_id=1, source_target_pairs={{0,4},{2,6},{4,0},{6,2},{8,12},{10,14},{12,8},{14,10},{16,20},{18,... | collective-permute-start | bytes 221192 | tf_op jit(solution)/shard_map/ppermute | solution.py:65
  35.0 4.4 %collective-permute-start.11 = (f32[144,128]{1,0:T(8,128)S(1)}, f32[144,128]{1,0:T(8,128)S(1)}, u32[]{:S(2)}, u32[]{:S(2)}) collective-permute-start(f32[144,128]{1,0:T(8,128)S(1)} %shard_map.129.refs_0_), channel_id=1, source_target_pairs={{0,2},{2,0},{4,6},{6,4},{8,10},{10,8},{12,14},{14,12},{16,18},{18,... | collective-permute-start | bytes 221192 | tf_op jit(solution)/shard_map/ppermute | solution.py:65
  39.3 1.3 %collective-permute-start.14 = (f32[144,128]{1,0:T(8,128)S(1)}, f32[144,128]{1,0:T(8,128)S(1)}, u32[]{:S(2)}, u32[]{:S(2)}) collective-permute-start(f32[144,128]{1,0:T(8,128)S(1)} %shard_map.130.refs_0_), channel_id=1, source_target_pairs={{0,1},{1,0},{2,3},{3,2},{4,5},{5,4},{6,7},{7,6},{8,9},{9,8},{10,11... | collective-permute-start | bytes 221192 | tf_op jit(solution)/shard_map/ppermute | solution.py:65
where the time goes:
time: 42 us; the launch traced here: 41.8 us
  starting transfers between devices  17.5 us (42%)
  waiting for transfers between devices  13.2 us (31%)
  Pallas kernels  10.4 us (25%)
  between operations  0.75 us (2%)
    ppermute x15, starting transfers between devices, swap(): return lax.ppermute(array, axis, pairs)  17.5 us
    ppermute x15, waiting for transfers between devices, swap(): return lax.ppermute(array, axis, pairs)  13.2 us
    pallas_call x12, Pallas kernels, call(): pl.pallas_call(kernel, out_shape=[jax.ShapeDtypeStruct(s, d) for s, d in...  10.4 us
  transfers between devices with their start and end apart: 15, of which 9 were waited for; matrix products, arithmetic and copies ran while one was open for 0% of the time, Pallas kernels for 14%

commit v1 on v0

--- a/solution.py
+++ b/solution.py
@@ -117,54 +117,55 @@
     return copies
 
 
-def mix_kernel(held, local, patch, mixes, ids_hbm, weights_hbm, lengths_hbm, src_hbm, *rest):
-    outs, (ids, weights, lengths, src, sems) = rest[:mixes], rest[mixes:]
-    copies = fetch((src_hbm, ids_hbm, weights_hbm, lengths_hbm), (src, ids, weights, lengths), sems)
+def local_kernel(held, patch, mixes, *refs):
+    inputs, outs, scratch = refs[:5], refs[5:10], refs[10:]
+    part_ref, factor_ref, gx_ref, fade_ref, row_ref = outs
+    src, forget, ids, weights, lengths, sems = scratch
+    copies = fetch(inputs, (src, forget, ids, weights, lengths), sems)
     me = lax.axis_index("mix")
-    _, high, lanes = outs[0].shape
+    local, high, lanes = part_ref.shape
+    _, heads, steps = forget.shape
+    s, t = rows_cols((steps, steps))
+    upto = (s <= t).astype(BF16)
     first = lax.axis_index("ctx") * (high * lanes // patch)
     row, col = rows_cols((high, lanes))
     position = first + row * (lanes // patch) + col // patch
     for copy in copies:
         copy.wait()
-    for slot in range(mixes):
-        target = other(me, mixes, slot)
-        for b in range(local):
-            total = jnp.zeros((high, lanes), F32)
-            for term in range(ids.shape[1]):
-                mixture = target * local + b
-                at = ids[mixture, term] - me * held
-                here = jnp.logical_and(at >= 0, at < held)
-                factor = jnp.where(here, weights[mixture, term], 0.0)
-                rows = src[pl.ds(jnp.where(here, at, 0), high, held), :]
-                total += jnp.where(position < lengths[mixture, term], factor, 0.0) * rows
-            outs[slot][b] = total
-
-
-def gate_kernel(patch, forget_hbm, gx_ref, fade_ref, row_ref, forget, sems):
-    copies = fetch((forget_hbm,), (forget,), sems)
-    local, heads, steps = forget.shape
-    lanes = heads * patch
-    s, t = rows_cols((steps, steps))
-    upto = (s <= t).astype(BF16)
-    for copy in copies:
-        copy.wait()
+    for b in range(local):
+        mixture = me * local + b
+        total = jnp.zeros((high, lanes), F32)
+        terms = []
+        for term in range(ids.shape[1]):
+            shown = jnp.where(position < lengths[mixture, term], weights[mixture, term], 0.0)
+            at = ids[mixture, term] - me * held
+            here = jnp.logical_and(at >= 0, at < held)
+            rows = src[pl.ds(jnp.where(here, at, 0), high, held), :]
+            total += jnp.where(here, shown, 0.0) * rows
+            terms.append((ids[mixture, term], shown))
+        part_ref[b] = total
+        for slot in range(1, mixes):
+            for source in range(held):
+                wanted = other(me, mixes, slot) * held + source
+                factor = jnp.zeros((high, lanes), F32)
+                for identity, shown in terms:
+                    factor += jnp.where(identity == wanted, shown, 0.0)
+                factor_ref[slot - 1, b, source] = factor
     for b in range(local):
         log_gate = jnp.log1p(forget[b] - 1.0)
-        high, low = halves(log_gate)
-        lowest = (log_gate - high.astype(F32) - low.astype(F32)).astype(BF16)
-        sums = quick(jnp.concatenate([high, low, lowest, jnp.zeros_like(low)], axis=0), upto)
+        high_half, low = halves(log_gate)
+        lowest = (log_gate - high_half.astype(F32) - low.astype(F32)).astype(BF16)
+        sums = quick(jnp.concatenate([high_half, low, lowest, jnp.zeros_like(low)], axis=0), upto)
         sums = sums[:heads] + sums[heads : 2 * heads] + sums[2 * heads : 3 * heads]
         row_ref[b * heads : (b + 1) * heads] = sums
-        wide = jnp.broadcast_to(sums[:, None, :], (heads, patch, steps)).reshape(lanes, steps)
+        wide = jnp.broadcast_to(sums[:, None, :], (heads, patch, steps)).reshape(-1, steps)
         gx = wide.T
         gx_ref[b] = gx
         fade_ref[b] = jnp.exp(gx[steps - 1 : steps] - gx)
 
 
-def gram_kernel(heads, patch, count, *refs):
-    parts, (gx, fade) = refs[:count], refs[count : count + 2]
-    mt_ref, pack_ref = refs[count + 2 :]
+def gram_kernel(held, patch, others, *refs):
+    sources, (part, factor, gx, fade, mt_ref, pack_ref) = refs[:others], refs[others:]
     local, steps, lanes = gx.shape
     per = lanes // patch
     t, r = rows_cols((local * steps, local * steps // per))
@@ -173,10 +174,14 @@
     chosen = t % per == lane // patch
     a, b_ = rows_cols((lanes, lanes))
     fold = (a % patch == b_ % patch).astype(BF16)
-    total = parts[0][...]
-    for part in parts[1:]:
-        total = total + part[...]
-    wide = quick(spread, total.reshape(local * steps // per, lanes))
+    totals = []
+    for b in range(local):
+        total = part[b]
+        for slot, source in enumerate(sources):
+            for s in range(held):
+                total += factor[slot, b, s] * source[pl.ds(s, steps // per, held), :]
+        totals.append(total)
+    wide = quick(spread, jnp.concatenate(totals, axis=0))
     mt = quick(jnp.where(chosen, wide, 0.0), fold)
     mt_ref[...] = mt.astype(BF16).reshape(mt_ref.shape)
     pack_ref[local * patch :] = jnp.zeros((pack_ref.shape[0] - local * patch, lanes), F32)
@@ -513,38 +518,38 @@
     rows_out = width // count
     per = count // heads
     dma = pltpu.SemaphoreType.DMA
-    partial_shape = (local, steps * patch // lanes, lanes)
-    panels = sources.reshape((held,) + partial_shape[1:]).transpose(1, 0, 2).reshape(-1, lanes)
-    partials = call(
-        functools.partial(mix_kernel, held, local, patch, mixes),
-        [(partial_shape, F32)] * mixes,
-        [source_ids, mix_weights, source_lengths, panels],
-        hbm=(0, 1, 2, 3),
+    subs = heads
+    sub = steps // subs
+    part_shape = (local, steps * patch // lanes, lanes)
+    panels = sources.reshape((held,) + part_shape[1:]).transpose(1, 0, 2).reshape(-1, lanes)
+    got = [swap(panels, "mix", 1, mixes, s) for s in range(1, mixes)]
+    part, factor, gx, fade, sums = call(
+        functools.partial(local_kernel, held, patch, mixes),
+        [
+            (part_shape, F32),
+            ((max(mixes - 1, 1), local, held) + part_shape[1:], F32),
+            ((local, steps, lanes), F32),
+            ((local, steps, lanes), F32),
+            ((local * heads, steps), F32),
+        ],
+        [panels, forget, source_ids, mix_weights, source_lengths],
+        hbm=(0, 1, 2, 3, 4),
+        flops=10**9,
         scratch=[
+            pltpu.VMEM(panels.shape, F32),
+            pltpu.VMEM(forget.shape, F32),
             pltpu.SMEM(source_ids.shape, jnp.int32),
             pltpu.SMEM(mix_weights.shape, F32),
             pltpu.SMEM(source_lengths.shape, jnp.int32),
-            pltpu.VMEM(panels.shape, F32),
-            dma((4,)),
-        ],
-    )
-    got = [partials[0]] + [swap(partials[s], "mix", 1, mixes, s) for s in range(1, mixes)]
-    subs = heads
-    sub = steps // subs
-    gx, fade, sums = call(
-        functools.partial(gate_kernel, patch),
-        [((local, steps, lanes), F32), ((local, steps, lanes), F32), ((local * heads, steps), F32)],
-        [forget],
-        hbm=(0,),
-        flops=10**8,
-        scratch=[pltpu.VMEM(forget.shape, F32), dma((1,))],
+            dma((5,)),
+        ],
     )
     high = -(-local // 8) * 8
     pack_shape = ((local * patch + high, lanes), F32)
     mt, pack = call(
-        functools.partial(gram_kernel, heads, patch, mixes),
+        functools.partial(gram_kernel, held, patch, len(got)),
         [((local, steps, lanes), BF16), pack_shape],
-        got + [gx, fade],
+        got + [part, factor, gx, fade],
     )
     a, m, c, keys, v, value_blocks, own, qkv_rows = call(
         functools.partial(weight_kernel, heads),

time: 42 us -> 41.3 us (0.983)
  Pallas kernels: 10.4 us -> 9.74 us
    pallas_call x12 -> x11, Pallas kernels: 10.4 us -> 9.74 us  [call(): pl.pallas_call(kernel, out_shape=[jax.ShapeDtypeStruct(s, d) for s, d in...]
  transfers between devices with their start and end apart: 15 -> 15, of which waited for: 9 -> 10; matrix products, arithmetic and copies ran while one was open for 0% -> 0% of each run, Pallas kernels for 14% -> 15%
where the time goes in v1:
time: 41.3 us; the launch traced here: 41.1 us
  starting transfers between devices  17.4 us (42%)
  waiting for transfers between devices  13.2 us (32%)
  Pallas kernels  9.74 us (24%)
  between operations  0.74 us (2%)
    ppermute x15, starting transfers between devices, swap(): return lax.ppermute(array, axis, pairs)  17.4 us
    ppermute x15, waiting for transfers between devices, swap(): return lax.ppermute(array, axis, pairs)  13.2 us
    pallas_call x11, Pallas kernels, call(): pl.pallas_call(kernel, out_shape=[jax.ShapeDtypeStruct(s, d) for s, d in...  9.74 us
  transfers between devices with their start and end apart: 15, of which 10 were waited for; matrix products, arithmetic and copies ran while one was open for 0% of the time, Pallas kernels for 15%

profile of v1, /device:TPU:0, one launch (start us, length us, event | category | flops | bytes accessed | tf_op | source)
XLA Modules:
  0.0 41.1 jit_solution(15827887969506395676)
XLA Ops:
  0.6 0.5 %collective-permute-start = (f32[256,128]{1,0:T(8,128)}, f32[256,128]{1,0:T(8,128)S(1)}, u32[]{:S(2)}, u32[]{:S(2)}) collective-permute-start(f32[256,128]{1,0:T(8,128)} %bitcast.6), channel_id=1, source_target_pairs={{0,1},{1,0},{2,3},{3,2},{4,5},{5,4},{6,7},{7,6},{8,9},{9,8},{10,11... | collective-permute-start | bytes 393224 | tf_op jit(solution)/shard_map/ppermute | solution.py:65
  1.1 1.4 %shard_map.120 = (f32[2,64,128]{2,1,0:T(8,128)S(1)}, f32[1,2,4,64,128]{4,3,2,1,0:T(8,128)S(1)}, f32[2,256,128]{2,1,0:T(8,128)S(1)}, f32[2,256,128]{2,1,0:T(8,128)S(1)}, f32[8,256]{1,0:T(8,128)S(1)}) custom-call(f32[256,128]{1,0:T(8,128)} %bitcast.7, f32[2,4,256]{2,1,0:T(4,128)} %refs_1_.2, s32[4,3]{1,0:T(4,128)} %refs_2_.1, f32[4,3]{1,0:T(4,128)} %refs_3_.1, ...), custom_call_target="tpu_custom_call" | custom-call | flops 1000000000 | bytes 1048576 | tf_op jit(solution)/shard_map/pallas_call | solution.py:76
  3.0 3.7 %collective-permute-start.3 = (f32[72,128]{1,0:T(8,128)S(1)}, f32[72,128]{1,0:T(8,128)S(1)}, u32[]{:S(2)}, u32[]{:S(2)}) collective-permute-start(f32[72,128]{1,0:T(8,128)S(1)} %get-tuple-element.46.refs_0_.refs_2_), channel_id=1, source_target_pairs={{0,6},{2,4},{4,2},{6,0},{8,14},{10,12},{12,10},{14,8},{16,22},{18,... | collective-permute-start | bytes 110600 | tf_op jit(solution)/shard_map/ppermute | solution.py:65
  6.7 0.5 %collective-permute-start.2 = (f32[72,128]{1,0:T(8,128)S(1)}, f32[72,128]{1,0:T(8,128)S(1)}, u32[]{:S(2)}, u32[]{:S(2)}) collective-permute-start(f32[72,128]{1,0:T(8,128)S(1)} %get-tuple-element.46.refs_0_.refs_2_), channel_id=1, source_target_pairs={{0,4},{2,6},{4,0},{6,2},{8,12},{10,14},{12,8},{14,10},{16,20},{18,... | collective-permute-start | bytes 110600 | tf_op jit(solution)/shard_map/ppermute | solution.py:65
  7.3 2.2 %shard_map.123 = (f32[32,1536]{1,0:T(8,128)S(1)}, bf16[256,256]{1,0:T(8,128)(2,1)S(1)}, bf16[256,256]{1,0:T(8,128)(2,1)S(1)}, bf16[384,512]{1,0:T(8,128)(2,1)S(1...) custom-call(bf16[32,512]{1,0:T(8,128)(2,1)} %bitcast.8, ...), custom_call_target="tpu_custom_call" | custom-call | flops 1000000000 | bytes 1048576 | tf_op jit(solution)/shard_map/pallas_call | solution.py:76
  9.6 1.1 %collective-permute-done.2.refs_2_ = f32[72,128]{1,0:T(8,128)S(1)} collective-permute-done((f32[72,128]{1,0:T(8,128)S(1)}, f32[72,128]{1,0:T(8,128)S(1)}, u32[]{:S(2)}, u32[]{:S(2)}) %collective-permute-start.2) | collective-permute-done | bytes 36896 | tf_op jit(solution)/shard_map/ppermute | solution.py:65
  11.2 3.7 %collective-permute-start.6 = (f32[72,128]{1,0:T(8,128)S(1)}, f32[72,128]{1,0:T(8,128)S(1)}, u32[]{:S(2)}, u32[]{:S(2)}) collective-permute-start(f32[72,128]{1,0:T(8,128)S(1)} %get-tuple-element.47._.refs_0_), channel_id=1, source_target_pairs={{0,24},{2,26},{4,28},{6,30},{8,16},{10,18},{12,20},{14,22},{16,8},... | collective-permute-start | bytes 110600 | tf_op jit(solution)/shard_map/ppermute | solution.py:65
  14.9 0.8 %collective-permute-start.4 = (f32[72,128]{1,0:T(8,128)S(1)}, f32[72,128]{1,0:T(8,128)S(1)}, u32[]{:S(2)}, u32[]{:S(2)}) collective-permute-start(f32[72,128]{1,0:T(8,128)S(1)} %get-tuple-element.47._.refs_0_), channel_id=1, source_target_pairs={{0,8},{2,10},{4,12},{6,14},{8,0},{10,2},{12,4},{14,6},{16,24},{18,... | collective-permute-start | bytes 110600 | tf_op jit(solution)/shard_map/ppermute | solution.py:65
  15.7 1.7 %shard_map.125 = (bf16[128,512]{1,0:T(8,128)(2,1)S(1)}, f32[2,256,128]{2,1,0:T(8,128)S(1)}, bf16[512,512]{1,0:T(8,128)(2,1)S(1)}, bf16[2,256,512]{2,1,0:T(8,128)(2,1)S(1)}) custom-call(bf16[512,512]{1,0:T(8,128)(2,1)} %out_hbm.1, bf16[2,256,512]{2,1,0:T(8,128)(2,1)} %cot_hbm.1, bf16[128,1024]{1,0:T(8,128)(2,1)S(1)} %get-tuple-element.59.vb, ...), custom_call_target="tpu_custom_call" | custom-call | flops 1000000000 | bytes 1048576 | tf_op jit(solution)/shard_map/pallas_call | solution.py:76
  17.4 0.9 %shard_map.124 = (f32[2,256,128]{2,1,0:T(8,128)S(1)}, bf16[2,256,128]{2,1,0:T(8,128)(2,1)S(1)}, f32[2,256,128]{2,1,0:T(8,128)S(1)}, bf16[2,4,256,128]{3,2,1,0:T(...) custom-call(bf16[2,256,128]{2,1,0:T(8,128)(2,1)S(1)} %get-tuple-element., ...), custom_call_target="tpu_custom_call" | custom-call | flops 1000000000 | bytes 1048576 | tf_op jit(solution)/shard_map/pallas_call | solution.py:76
  18.3 1.5 %collective-permute-done.5.refs_2_ = f32[72,128]{1,0:T(8,128)S(1)} collective-permute-done((f32[72,128]{1,0:T(8,128)S(1)}, f32[72,128]{1,0:T(8,128)S(1)}, u32[]{:S(2)}, u32[]{:S(2)}) %collective-permute-start.5) | collective-permute-done | bytes 36896 | tf_op jit(solution)/shard_map/ppermute | solution.py:65
  19.7 1.8 %shard_map.126 = (bf16[2,256,512]{2,1,0:T(8,128)(2,1)}, f32[336,128]{1,0:T(8,128)S(1)}, f32[336,128]{1,0:T(8,128)S(1)}) custom-call(f32[72,128]{1,0:T(8,128)S(1)} %get-tuple-element.47._.refs_0_, f32[72,128]{1,0:T(8,128)S(1)} %collective-permute-done.4.refs_1_, f32[72,128]{1,0:T(8,128)S(1)} %collective-permute-done.5.refs_2_, ...), custom_call_target="tpu_custom_call" | custom-call | flops 1000000000 | bytes 1048576 | tf_op jit(solution)/shard_map/pallas_call | solution.py:76
  21.7 1.4 %collective-permute-done.7.refs_1_ = f32[336,128]{1,0:T(8,128)S(1)} collective-permute-done((f32[336,128]{1,0:T(8,128)S(1)}, f32[336,128]{1,0:T(8,128)S(1)}, u32[]{:S(2)}, u32[]{:S(2)}) %collective-permute-start.7) | collective-permute-done | bytes 172064 | tf_op jit(solution)/shard_map/ppermute | solution.py:65
  23.2 2.7 %collective-permute-start.9 = (f32[144,128]{1,0:T(8,128)S(1)}, f32[144,128]{1,0:T(8,128)S(1)}, u32[]{:S(2)}, u32[]{:S(2)}) collective-permute-start(f32[144,128]{1,0:T(8,128)S(1)} %get-tuple-element.71), channel_id=1, source_target_pairs={{0,16},{2,18},{4,20},{6,22},{8,24},{10,26},{12,28},{14,30},{16,0},... | collective-permute-start | bytes 221192 | tf_op jit(solution)/shard_map/ppermute | solution.py:65
  25.9 1.6 %collective-permute-start.10 = (f32[144,128]{1,0:T(8,128)S(1)}, f32[144,128]{1,0:T(8,128)S(1)}, u32[]{:S(2)}, u32[]{:S(2)}) collective-permute-start(f32[144,128]{1,0:T(8,128)S(1)} %get-tuple-element.72), channel_id=1, source_target_pairs={{0,24},{2,26},{4,28},{6,30},{8,16},{10,18},{12,20},{14,22},{16,8},... | collective-permute-start | bytes 221192 | tf_op jit(solution)/shard_map/ppermute | solution.py:65
  27.6 1.5 %collective-permute-done.8.refs_1_ = f32[144,128]{1,0:T(8,128)S(1)} collective-permute-done((f32[144,128]{1,0:T(8,128)S(1)}, f32[144,128]{1,0:T(8,128)S(1)}, u32[]{:S(2)}, u32[]{:S(2)}) %collective-permute-start.8) | collective-permute-done | bytes 73760 | tf_op jit(solution)/shard_map/ppermute | solution.py:65
  29.1 3.0 %collective-permute-done.10.refs_3_ = f32[144,128]{1,0:T(8,128)S(1)} collective-permute-done((f32[144,128]{1,0:T(8,128)S(1)}, f32[144,128]{1,0:T(8,128)S(1)}, u32[]{:S(2)}, u32[]{:S(2)}) %collective-permute-start.10) | collective-permute-done | bytes 73760 | tf_op jit(solution)/shard_map/ppermute | solution.py:65
  32.2 1.6 %collective-permute-start.13 = (f32[144,128]{1,0:T(8,128)S(1)}, f32[144,128]{1,0:T(8,128)S(1)}, u32[]{:S(2)}, u32[]{:S(2)}) collective-permute-start(f32[144,128]{1,0:T(8,128)S(1)} %shard_map.128.refs_0_), channel_id=1, source_target_pairs={{0,6},{2,4},{4,2},{6,0},{8,14},{10,12},{12,10},{14,8},{16,22},{18,... | collective-permute-start | bytes 221192 | tf_op jit(solution)/shard_map/ppermute | solution.py:65
  33.7 0.5 %collective-permute-start.12 = (f32[144,128]{1,0:T(8,128)S(1)}, f32[144,128]{1,0:T(8,128)S(1)}, u32[]{:S(2)}, u32[]{:S(2)}) collective-permute-start(f32[144,128]{1,0:T(8,128)S(1)} %shard_map.128.refs_0_), channel_id=1, source_target_pairs={{0,4},{2,6},{4,0},{6,2},{8,12},{10,14},{12,8},{14,10},{16,20},{18,... | collective-permute-start | bytes 221192 | tf_op jit(solution)/shard_map/ppermute | solution.py:65
  34.2 1.5 %collective-permute-start.11 = (f32[144,128]{1,0:T(8,128)S(1)}, f32[144,128]{1,0:T(8,128)S(1)}, u32[]{:S(2)}, u32[]{:S(2)}) collective-permute-start(f32[144,128]{1,0:T(8,128)S(1)} %shard_map.128.refs_0_), channel_id=1, source_target_pairs={{0,2},{2,0},{4,6},{6,4},{8,10},{10,8},{12,14},{14,12},{16,18},{18,... | collective-permute-start | bytes 221192 | tf_op jit(solution)/shard_map/ppermute | solution.py:65
  35.7 2.2 %collective-permute-done.13.refs_3_ = f32[144,128]{1,0:T(8,128)S(1)} collective-permute-done((f32[144,128]{1,0:T(8,128)S(1)}, f32[144,128]{1,0:T(8,128)S(1)}, u32[]{:S(2)}, u32[]{:S(2)}) %collective-permute-start.13) | collective-permute-done | bytes 73760 | tf_op jit(solution)/shard_map/ppermute | solution.py:65
  37.9 0.6 %collective-permute-done.12.refs_2_ = f32[144,128]{1,0:T(8,128)S(1)} collective-permute-done((f32[144,128]{1,0:T(8,128)S(1)}, f32[144,128]{1,0:T(8,128)S(1)}, u32[]{:S(2)}, u32[]{:S(2)}) %collective-permute-start.12) | collective-permute-done | bytes 73760 | tf_op jit(solution)/shard_map/ppermute | solution.py:65
  38.7 1.3 %collective-permute-done.14.refs_1_ = f32[144,128]{1,0:T(8,128)S(1)} collective-permute-done((f32[144,128]{1,0:T(8,128)S(1)}, f32[144,128]{1,0:T(8,128)S(1)}, u32[]{:S(2)}, u32[]{:S(2)}) %collective-permute-start.14) | collective-permute-done | bytes 73760 | tf_op jit(solution)/shard_map/ppermute | solution.py:65
  39.9 1.1 %shard_map.130 = (f32[32,1536]{1,0:T(8,128)}, f32[32,512]{1,0:T(8,128)}, f32[32,32]{1,0:T(8,128)}) custom-call(f32[144,128]{1,0:T(8,128)S(1)} %shard_map.129.refs_0_, f32[144,128]{1,0:T(8,128)S(1)} %collective-permute-done.14.refs_1_, f32[32,1536]{1,0:T(8,128)S(1)} %get-tuple-element.73.refs_2_, bf16[384,512]{1,0:T(8,128)(2,1)S(1)} %get-tuple-element.74.refs_3_, ...), custom_call_target="tpu_custom_call" | custom-call | bytes 1048576 | tf_op jit(solution)/shard_map/pallas_call | solution.py:76
  (17 shorter events, 1.5 us)
Async XLA Ops:
  0.6 1.9 %collective-permute-start = (f32[256,128]{1,0:T(8,128)}, f32[256,128]{1,0:T(8,128)S(1)}, u32[]{:S(2)}, u32[]{:S(2)}) collective-permute-start(f32[256,128]{1,0:T(8,128)} %bitcast.6), channel_id=1, source_target_pairs={{0,1},{1,0},{2,3},{3,2},{4,5},{5,4},{6,7},{7,6},{8,9},{9,8},{10,11... | collective-permute-start | bytes 393224 | tf_op jit(solution)/shard_map/ppermute | solution.py:65
  3.0 6.5 %collective-permute-start.3 = (f32[72,128]{1,0:T(8,128)S(1)}, f32[72,128]{1,0:T(8,128)S(1)}, u32[]{:S(2)}, u32[]{:S(2)}) collective-permute-start(f32[72,128]{1,0:T(8,128)S(1)} %get-tuple-element.46.refs_0_.refs_2_), channel_id=1, source_target_pairs={{0,6},{2,4},{4,2},{6,0},{8,14},{10,12},{12,10},{14,8},{16,22},{18,... | collective-permute-start | bytes 110600 | tf_op jit(solution)/shard_map/ppermute | solution.py:65
  6.7 4.0 %collective-permute-start.2 = (f32[72,128]{1,0:T(8,128)S(1)}, f32[72,128]{1,0:T(8,128)S(1)}, u32[]{:S(2)}, u32[]{:S(2)}) collective-permute-start(f32[72,128]{1,0:T(8,128)S(1)} %get-tuple-element.46.refs_0_.refs_2_), channel_id=1, source_target_pairs={{0,4},{2,6},{4,0},{6,2},{8,12},{10,14},{12,8},{14,10},{16,20},{18,... | collective-permute-start | bytes 110600 | tf_op jit(solution)/shard_map/ppermute | solution.py:65
  7.2 4.0 %collective-permute-start.1 = (f32[72,128]{1,0:T(8,128)S(1)}, f32[72,128]{1,0:T(8,128)S(1)}, u32[]{:S(2)}, u32[]{:S(2)}) collective-permute-start(f32[72,128]{1,0:T(8,128)S(1)} %get-tuple-element.46.refs_0_.refs_2_), channel_id=1, source_target_pairs={{0,2},{2,0},{4,6},{6,4},{8,10},{10,8},{12,14},{14,12},{16,18},{18,... | collective-permute-start | bytes 110600 | tf_op jit(solution)/shard_map/ppermute | solution.py:65
  11.2 7.1 %collective-permute-start.6 = (f32[72,128]{1,0:T(8,128)S(1)}, f32[72,128]{1,0:T(8,128)S(1)}, u32[]{:S(2)}, u32[]{:S(2)}) collective-permute-start(f32[72,128]{1,0:T(8,128)S(1)} %get-tuple-element.47._.refs_0_), channel_id=1, source_target_pairs={{0,24},{2,26},{4,28},{6,30},{8,16},{10,18},{12,20},{14,22},{16,8},... | collective-permute-start | bytes 110600 | tf_op jit(solution)/shard_map/ppermute | solution.py:65
  14.9 4.9 %collective-permute-start.5 = (f32[72,128]{1,0:T(8,128)S(1)}, f32[72,128]{1,0:T(8,128)S(1)}, u32[]{:S(2)}, u32[]{:S(2)}) collective-permute-start(f32[72,128]{1,0:T(8,128)S(1)} %get-tuple-element.47._.refs_0_), channel_id=1, source_target_pairs={{0,16},{2,18},{4,20},{6,22},{8,24},{10,26},{12,28},{14,30},{16,0},... | collective-permute-start | bytes 110600 | tf_op jit(solution)/shard_map/ppermute | solution.py:65
  14.9 4.9 %collective-permute-start.4 = (f32[72,128]{1,0:T(8,128)S(1)}, f32[72,128]{1,0:T(8,128)S(1)}, u32[]{:S(2)}, u32[]{:S(2)}) collective-permute-start(f32[72,128]{1,0:T(8,128)S(1)} %get-tuple-element.47._.refs_0_), channel_id=1, source_target_pairs={{0,8},{2,10},{4,12},{6,14},{8,0},{10,2},{12,4},{14,6},{16,24},{18,... | collective-permute-start | bytes 110600 | tf_op jit(solution)/shard_map/ppermute | solution.py:65
  21.6 1.5 %collective-permute-start.7 = (f32[336,128]{1,0:T(8,128)S(1)}, f32[336,128]{1,0:T(8,128)S(1)}, u32[]{:S(2)}, u32[]{:S(2)}) collective-permute-start(f32[336,128]{1,0:T(8,128)S(1)} %get-tuple-element.68), channel_id=1, source_target_pairs={{0,1},{1,0},{2,3},{3,2},{4,5},{5,4},{6,7},{7,6},{8,9},{9,8},{10,11... | collective-permute-start | bytes 516104 | tf_op jit(solution)/shard_map/ppermute | solution.py:65
  23.1 6.0 %collective-permute-start.8 = (f32[144,128]{1,0:T(8,128)S(1)}, f32[144,128]{1,0:T(8,128)S(1)}, u32[]{:S(2)}, u32[]{:S(2)}) collective-permute-start(f32[144,128]{1,0:T(8,128)S(1)} %get-tuple-element.70), channel_id=1, source_target_pairs={{0,8},{2,10},{4,12},{6,14},{8,0},{10,2},{12,4},{14,6},{16,24},{18,... | collective-permute-start | bytes 221192 | tf_op jit(solution)/shard_map/ppermute | solution.py:65
  23.2 5.9 %collective-permute-start.9 = (f32[144,128]{1,0:T(8,128)S(1)}, f32[144,128]{1,0:T(8,128)S(1)}, u32[]{:S(2)}, u32[]{:S(2)}) collective-permute-start(f32[144,128]{1,0:T(8,128)S(1)} %get-tuple-element.71), channel_id=1, source_target_pairs={{0,16},{2,18},{4,20},{6,22},{8,24},{10,26},{12,28},{14,30},{16,0},... | collective-permute-start | bytes 221192 | tf_op jit(solution)/shard_map/ppermute | solution.py:65
  25.9 6.2 %collective-permute-start.10 = (f32[144,128]{1,0:T(8,128)S(1)}, f32[144,128]{1,0:T(8,128)S(1)}, u32[]{:S(2)}, u32[]{:S(2)}) collective-permute-start(f32[144,128]{1,0:T(8,128)S(1)} %get-tuple-element.72), channel_id=1, source_target_pairs={{0,24},{2,26},{4,28},{6,30},{8,16},{10,18},{12,20},{14,22},{16,8},... | collective-permute-start | bytes 221192 | tf_op jit(solution)/shard_map/ppermute | solution.py:65
  32.2 5.8 %collective-permute-start.13 = (f32[144,128]{1,0:T(8,128)S(1)}, f32[144,128]{1,0:T(8,128)S(1)}, u32[]{:S(2)}, u32[]{:S(2)}) collective-permute-start(f32[144,128]{1,0:T(8,128)S(1)} %shard_map.128.refs_0_), channel_id=1, source_target_pairs={{0,6},{2,4},{4,2},{6,0},{8,14},{10,12},{12,10},{14,8},{16,22},{18,... | collective-permute-start | bytes 221192 | tf_op jit(solution)/shard_map/ppermute | solution.py:65
  33.7 4.8 %collective-permute-start.12 = (f32[144,128]{1,0:T(8,128)S(1)}, f32[144,128]{1,0:T(8,128)S(1)}, u32[]{:S(2)}, u32[]{:S(2)}) collective-permute-start(f32[144,128]{1,0:T(8,128)S(1)} %shard_map.128.refs_0_), channel_id=1, source_target_pairs={{0,4},{2,6},{4,0},{6,2},{8,12},{10,14},{12,8},{14,10},{16,20},{18,... | collective-permute-start | bytes 221192 | tf_op jit(solution)/shard_map/ppermute | solution.py:65
  34.2 4.4 %collective-permute-start.11 = (f32[144,128]{1,0:T(8,128)S(1)}, f32[144,128]{1,0:T(8,128)S(1)}, u32[]{:S(2)}, u32[]{:S(2)}) collective-permute-start(f32[144,128]{1,0:T(8,128)S(1)} %shard_map.128.refs_0_), channel_id=1, source_target_pairs={{0,2},{2,0},{4,6},{6,4},{8,10},{10,8},{12,14},{14,12},{16,18},{18,... | collective-permute-start | bytes 221192 | tf_op jit(solution)/shard_map/ppermute | solution.py:65
  38.6 1.3 %collective-permute-start.14 = (f32[144,128]{1,0:T(8,128)S(1)}, f32[144,128]{1,0:T(8,128)S(1)}, u32[]{:S(2)}, u32[]{:S(2)}) collective-permute-start(f32[144,128]{1,0:T(8,128)S(1)} %shard_map.129.refs_0_), channel_id=1, source_target_pairs={{0,1},{1,0},{2,3},{3,2},{4,5},{5,4},{6,7},{7,6},{8,9},{9,8},{10,11... | collective-permute-start | bytes 221192 | tf_op jit(solution)/shard_map/ppermute | solution.py:65
